TPU v7x, 32 devices: a whole 2x2x4 slice. The times are simulated.
32 devices in a mesh: groups: 2 (over x), goal: 16 (over z, y, core).
Axes of the slice: x: 2, y: 2, z: 4, core: 2. Of those that a mesh axis runs over, the one named last changes fastest.
Arguments:
- queries: bfloat16 [128, 64, 4096], P(('groups', 'goal')), parts along dimension 0, may hold values from -8 to 8
- goal_keys: bfloat16 [32, 256, 4096], P(('groups', 'goal')), parts along dimension 0, may hold values from -8 to 8
- goal_values: bfloat16 [32, 256, 4096], P(('groups', 'goal')), parts along dimension 0, may hold values from -6 to 6
- out_weight: bfloat16 [4096, 2048], P('goal'), may hold values from -0.5 to 0.5
- tactic_goal: int32 [128, 1], P(('groups', 'goal')), parts along dimension 0, may hold values from 0 to 15
- tactic_len: int32 [128], P(('groups', 'goal')), parts along dimension 0, may hold values from 1 to 64
Outputs:
- projected: bfloat16 [128, 64, 2048], P(('groups', 'goal')), parts along dimension 0
There are 2 independent parts, one for each index of `groups`. A program takes and returns all parts, laid end to end along the dimension named above; an argument that names none is the same for every part. Nothing has to cross between parts.
Inputs may be any that keep to these rules, and one draw needn't show every extreme that they name: `tactic_goal`: every goal is read by at least one tactic; tactics per goal are uneven. `tactic_len`: the live positions of a tactic are its leading ones.
All inputs are finite; a program needn't handle non-finite values.
Results may differ from a plain program's by a relative error of at most 0.01.
Values may be sent and summed in bfloat16 or wider, within the bound.
A program may use at most 192 MiB of HBM per device.

v0:
```python
import math
import jax
import jax.numpy as jnp
from jax import lax
from jax.sharding import PartitionSpec as P

DH = 64


def attend_block(query_block, keys_heads, values_heads, block_ids):
    tact_count = query_block.shape[0]
    row_count = query_block.shape[1]
    width_local = query_block.shape[2]
    head_count = width_local // DH
    keys_tact = jnp.take(keys_heads, block_ids, axis=0).reshape(tact_count, -1, head_count, DH)
    vals_tact = jnp.take(values_heads, block_ids, axis=0).reshape(tact_count, -1, head_count, DH)
    query_four = query_block.reshape(tact_count, row_count, head_count, DH)
    scores = jnp.einsum(
        "tihd,tjhd->thij", query_four, keys_tact, preferred_element_type=jnp.float32
    )
    biggest = jnp.max(scores, axis=-1, keepdims=True)
    powers = jnp.exp(scores - biggest)
    weights = (powers / jnp.sum(powers, axis=-1, keepdims=True)).astype(jnp.bfloat16)
    attended = jnp.einsum("thij,tjhd->tihd", weights, vals_tact, preferred_element_type=jnp.float32)
    return attended.reshape(tact_count, row_count, width_local).astype(jnp.bfloat16)


def attend(query_piece, keys_heads, values_heads, goal_ids):
    tact_count = query_piece.shape[0]
    row_count = query_piece.shape[1]
    width_local = query_piece.shape[2]
    block_size = math.gcd(tact_count, 64)
    block_count = tact_count // block_size
    query_blocks = query_piece.reshape(block_count, block_size, row_count, width_local)
    id_blocks = goal_ids.reshape(block_count, block_size)

    def one_block(operands):
        return attend_block(operands[0], keys_heads, values_heads, operands[1])

    results = lax.map(one_block, (query_blocks, id_blocks))
    return results.reshape(tact_count, row_count, width_local)


def shards(queries, goal_keys, goal_values, out_weight, tactic_goal, tactic_len):
    goal_ids = lax.all_gather(tactic_goal[:, 0], "goal", axis=0, tiled=True)
    keys_heads, values_heads = (
        lax.all_to_all(goal_keys, "goal", split_axis=2, concat_axis=0, tiled=True),
        lax.all_to_all(goal_values, "goal", split_axis=2, concat_axis=0, tiled=True),
    )
    query_heads = lax.all_to_all(queries, "goal", split_axis=2, concat_axis=0, tiled=True)
    attended = attend(query_heads, keys_heads, values_heads, goal_ids)
    merged = lax.all_to_all(attended, "goal", split_axis=0, concat_axis=2, tiled=True)
    live_rows = jnp.arange(merged.shape[1])[None, :] < tactic_len[:, None]
    context = jnp.where(live_rows[:, :, None], merged, jnp.zeros_like(merged))
    tact_local = context.shape[0]
    row_count = context.shape[1]
    flat = context.reshape(tact_local * row_count, context.shape[2])
    projected = jnp.dot(
        flat,
        lax.all_gather(out_weight, "goal", axis=0, tiled=True),
        preferred_element_type=jnp.float32,
    )
    return projected.astype(jnp.bfloat16).reshape(tact_local, row_count, out_weight.shape[1])


def solution(mesh):
    return jax.shard_map(
        shards,
        mesh=mesh,
        in_specs=(
            P(("groups", "goal"), None, None),
            P(("groups", "goal"), None, None),
            P(("groups", "goal"), None, None),
            P("goal", None),
            P(("groups", "goal"), None),
            P(("groups", "goal")),
        ),
        out_specs=P(("groups", "goal"), None, None),
        check_vma=False,
    )
```

profile of v0, /device:TPU:13, one launch (start us, length us, event | category | flops | bytes accessed | tf_op | source)
XLA Modules:
  0.0 509.1 jit_solution(2314349538631211243)
XLA Ops:
  6.5 0.7 all-gather.3.cloned.1.call-update
  7.3 10.1 %copy.23 = bf16[1,256,4096]{1,0,2:T(2,128)(2,1)} copy(bf16[1,256,4096]{2,1,0:T(8,128)(2,1)} %param.10) | data formatting | bytes 4194304 | tf_op args[2]
  17.3 0.5 broadcast.32
  17.8 21.7 %reduce.1 = bf16[4096,256]{1,0:T(8,128)(2,1)S(1)} reduce(bf16[4096,1,256]{2,1,0:T(2,128)(2,1)} %bitcast.58, bf16[]{:T(256)} %broadcast.32), dimensions={1}, to_apply=%bitcast.44.reduce_sub_computation | reduce | bytes 4194306
  39.5 2.1 reshape.91
  41.6 6.6 %all-to-all-start = ((bf16[16,2,32768]{2,1,0:T(2,128)(2,1)}), bf16[16,2,32768]{2,1,0:T(2,128)(2,1)S(1)}, u32[]{:S(2)}, u32[]{:S(2)}) async-start(bf16[16,2,32768]{2,1,0:T(2,128)(2,1)} %reshape.91), calls=%async_computation | async-start | bytes 4194304 | tf_op jit(solution)/shard_map/all_to_all | solution.py:48
  48.1 10.1 %copy.26 = bf16[1,256,4096]{1,0,2:T(2,128)(2,1)} copy(bf16[1,256,4096]{2,1,0:T(8,128)(2,1)} %param.9) | data formatting | bytes 4194304 | tf_op args[1]
  58.2 23.0 %reduce = bf16[4096,256]{1,0:T(8,128)(2,1)} reduce(bf16[4096,1,256]{2,1,0:T(2,128)(2,1)} %bitcast.59, bf16[]{:T(256)} %broadcast.32), dimensions={1}, to_apply=%bitcast.46.reduce_sub_computation | reduce | bytes 4194306
  81.1 4.0 reshape.93
  85.1 58.2 %all-to-all-done = bf16[16,2,32768]{2,1,0:T(2,128)(2,1)S(1)} async-done(((bf16[16,2,32768]{2,1,0:T(2,128)(2,1)}), bf16[16,2,32768]{2,1,0:T(2,128)(2,1)S(1)}, u32[]{:S(2)}, u32[]{:S(2)}) %all-to-all-start) | async-done | bytes 2097184 | tf_op jit(solution)/shard_map/all_to_all | solution.py:48
  143.3 4.3 all-to-all-start.1
  147.7 0.0 copy-start.2
  147.7 0.0 copy-start
  147.7 7.0 %copy.29 = bf16[4,64,4096]{1,0,2:T(4,128)(2,1)} copy(bf16[4,64,4096]{2,1,0:T(8,128)(2,1)} %param.8) | data formatting | bytes 4194304 | tf_op args[0]
  154.7 7.5 %reshape.95 = bf16[16,2,32768]{2,1,0:T(2,128)(2,1)} reshape(bf16[4096,4,64]{2,1,0:T(4,128)(2,1)} %bitcast.63) | data formatting | bytes 4194304
  162.3 52.0 %all-to-all-done.1 = bf16[16,2,32768]{2,1,0:T(2,128)(2,1)} async-done(((bf16[16,2,32768]{2,1,0:T(2,128)(2,1)}), bf16[16,2,32768]{2,1,0:T(2,128)(2,1)}, u32[]{:S(2)}, u32[]{:S(2)}) %all-to-all-start.1) | async-done | bytes 2097184 | tf_op jit(solution)/shard_map/all_to_all | solution.py:47
  214.3 4.7 all-to-all-start.2
  219.0 0.0 copy-done.2
  219.0 0.6 dynamic-slice.1
  220.3 0.1 bitcast_dynamic-update-slice_fusion
  220.4 44.1 %all-reduce = s32[64]{0:T(128)S(1)} all-reduce(s32[64]{0:T(128)S(1)} %bitcast_dynamic-update-slice_fusion), channel_id=2, replica_groups=mesh['groups'=2,'goal'=16] {'goal'}, use_global_device_ids=true, to_apply=%add | all-reduce | flops 64 | bytes 512 | tf_op jit(solution)/shard_map/all_gather | solution.py:45
  264.5 6.8 %reshape.92 = bf16[4096,1,256]{2,1,0:T(2,128)(2,1)} reshape(bf16[16,2,32768]{2,1,0:T(2,128)(2,1)S(1)} %all-to-all-done) | data formatting | bytes 4194304
  271.3 3.9 copy.34
  275.1 2.8 copy.24
  278.0 10.5 %reshape.94 = bf16[4096,1,256]{2,1,0:T(2,128)(2,1)} reshape(bf16[16,2,32768]{2,1,0:T(2,128)(2,1)} %all-to-all-done.1) | data formatting | bytes 4194304
  288.5 3.9 copy.35
  292.4 3.9 copy.27
  296.3 5.5 %gather_fusion = bf16[64,256,256]{2,1,0:T(8,128)(2,1)} fusion(bf16[16,256,256]{2,1,0:T(8,128)(2,1)S(1)} %bitcast.56, s32[1024]{0:T(1024)S(1)} %pad_clamp_fusion), kind=kCustom, calls=%fused_computation.clone | custom fusion | bytes 16777472 | tf_op jit(solution)/shard_map/while/body/eval_jaxpr/jit(_take)/gather | solution.py:16
  301.8 7.1 %gather_fusion.1 = bf16[64,256,256]{2,1,0:T(8,128)(2,1)} fusion(bf16[16,256,256]{2,1,0:T(8,128)(2,1)} %bitcast.57, s32[1024]{0:T(1024)S(1)} %pad_clamp_fusion), kind=kCustom, calls=%fused_computation.1.clone | custom fusion | bytes 16777472 | tf_op jit(solution)/shard_map/while/body/eval_jaxpr/jit(_take)/gather | solution.py:15
  308.9 11.6 %broadcast_select_fusion = (bf16[64,256,256]{2,1,0:T(8,128)(2,1)}, bf16[64,256,256]{2,1,0:T(8,128)(2,1)}) fusion(bf16[64,256,256]{2,1,0:T(8,128)(2,1)} %gather_fusion.1, pred[64]{0:T(512)(128)(4,1)S(1)} %compare_and_fusion, bf16[64,256,256]{2,1,0:T(8,128)(2,1)} %gather_fusion), kind=kLoop, calls=%fused_computation.9 | loop fusion | flops 8388608 | bytes 33554496 | tf_op jit(solution)/shard_map/while/body/eval_jaxpr/jit(_take)/select_n | solution.py:15
  320.5 11.9 %copy.28 = bf16[64,256,256]{1,2,0:T(8,128)(2,1)} copy(bf16[64,256,256]{2,1,0:T(8,128)(2,1)} %get-tuple-element.16) | data formatting | bytes 16777216 | tf_op jit(solution)/shard_map/while/body/eval_jaxpr/jit(_take)/select_n | solution.py:15
  332.4 0.0 all-to-all-done.2
  332.4 7.5 %reshape.96 = bf16[4096,4,64]{2,1,0:T(4,128)(2,1)} reshape(bf16[16,2,32768]{2,1,0:T(2,128)(2,1)} %all-to-all-done.2) | data formatting | bytes 4194304
  339.9 5.4 %copy.30 = bf16[4,64,16,256]{3,1,0,2:T(8,128)(2,1)S(1)} copy(bf16[4,64,16,256]{1,0,3,2:T(4,128)(2,1)} %bitcast.62) | data formatting | bytes 4194304 | tf_op jit(solution)/shard_map/all_to_all | solution.py:50
  345.2 3.3 reshape.60
  348.5 11.9 %copy.25 = bf16[64,256,256]{1,2,0:T(8,128)(2,1)} copy(bf16[64,256,256]{2,1,0:T(8,128)(2,1)} %get-tuple-element.17) | data formatting | bytes 16777216 | tf_op jit(solution)/shard_map/while/body/eval_jaxpr/jit(_take)/select_n | solution.py:16
  360.4 12.7 %fusion.6 = f32[64,4,256,64]{2,3,1,0:T(8,128)} fusion(bf16[64,256,4,64]{1,3,2,0:T(8,128)(2,1)} %bitcast.55, bf16[64,64,4,64]{3,2,1,0:T(4,128)(2,1)} %reshape.60), kind=kOutput, calls=%fused_computation.11 | convolution fusion | flops 536870912 | bytes 27262976 | tf_op jit(solution)/shard_map/while/body/eval_jaxpr/tihd,tjhd->thij/dot_general | solution.py:18
  373.1 14.6 %fusion.18 = f32[64,4,64]{2,1,0:T(4,128)S(1)} fusion(f32[64,4,256,64]{2,3,1,0:T(8,128)} %fusion.6), kind=kOutput, calls=%fused_computation.25 | output fusion | flops 8388863 | bytes 16842752 | tf_op jit(solution)/shard_map/while/body/eval_jaxpr/sub | solution.py:22
  387.7 43.3 %fusion.8 = bf16[64,4,64,64]{3,2,1,0:T(8,128)(2,1)} fusion(bf16[64,256,4,64]{1,3,2,0:T(8,128)(2,1)} %bitcast.67, f32[64,4,64]{2,1,0:T(4,128)S(1)} %fusion.18, f32[64,4,256,64]{2,3,1,0:T(8,128)} %fusion.6), kind=kOutput, calls=%fused_computation.13 | convolution fusion | flops 550519040 | bytes 27328512 | tf_op jit(solution)/shard_map/while/body/eval_jaxpr/thij,tjhd->tihd/dot_general | solution.py:24
  431.1 4.8 copy.32
  435.9 7.5 %all-to-all-start.3 = ((bf16[64,64,256]{2,1,0:T(8,128)(2,1)}), bf16[64,64,256]{2,1,0:T(8,128)(2,1)S(1)}, u32[]{:S(2)}, u32[]{:S(2)}) async-start(bf16[64,64,256]{2,1,0:T(8,128)(2,1)} %copy.32), calls=%async_computation.3 | async-start | bytes 4194304 | tf_op jit(solution)/shard_map/all_to_all | solution.py:52
  443.4 0.1 iota_compare_fusion
  443.5 0.1 lt.30
  443.6 47.3 %all-to-all-done.3 = bf16[64,64,256]{2,1,0:T(8,128)(2,1)S(1)} async-done(((bf16[64,64,256]{2,1,0:T(8,128)(2,1)}), bf16[64,64,256]{2,1,0:T(8,128)(2,1)S(1)}, u32[]{:S(2)}, u32[]{:S(2)}) %all-to-all-start.3) | async-done | bytes 2097184 | tf_op jit(solution)/shard_map/all_to_all | solution.py:52
  490.8 1.2 copy.33
  492.0 0.9 copy.36
  492.9 0.0 all-gather.3.cloned.1.call-done
  493.0 9.3 %convolution_convert_fusion = bf16[256,2048]{1,0:T(8,128)(2,1)} fusion(bf16[4096,2048]{1,0:T(8,128)(2,1)} %all-gather.3.cloned.1.call-done, bf16[256,4096]{1,0:T(8,128)(2,1)S(1)} %bitcast.71, pred[256]{0:T(512)(128)(4,1)S(1)} %lt.30), kind=kOutput, calls=%fused_computation.14 | convolution fusion | flops 4296540160 | bytes 19923200 | tf_op jit(solution)/shard_map/dot_general | solution.py:58
  (8 shorter events, 0.0 us)
Async XLA Ops:
  6.5 486.4 %all-gather.3.cloned.1.call-start = ((), (), s32[]{:S(2)}) async-start(), calls=%async_computation.4 | async-start | bytes 17825792 | tf_op jit(solution)/shard_map/all_gather | solution.py:60
  41.6 101.8 %all-to-all-start = ((bf16[16,2,32768]{2,1,0:T(2,128)(2,1)}), bf16[16,2,32768]{2,1,0:T(2,128)(2,1)S(1)}, u32[]{:S(2)}, u32[]{:S(2)}) async-start(bf16[16,2,32768]{2,1,0:T(2,128)(2,1)} %reshape.91), calls=%async_computation | async-start | bytes 4194304 | tf_op jit(solution)/shard_map/all_to_all | solution.py:48
  143.3 71.0 %all-to-all-start.1 = ((bf16[16,2,32768]{2,1,0:T(2,128)(2,1)}), bf16[16,2,32768]{2,1,0:T(2,128)(2,1)}, u32[]{:S(2)}, u32[]{:S(2)}) async-start(bf16[16,2,32768]{2,1,0:T(2,128)(2,1)} %reshape.93), calls=%async_computation.1 | async-start | bytes 4194304 | tf_op jit(solution)/shard_map/all_to_all | solution.py:47
  147.7 71.4 %copy-start.2 = (u32[32]{0:T(128)S(1)}, u32[32]{0:T(128)}, u32[]{:S(2)}) copy-start(u32[32]{0:T(128)} %constant.37) | copy-start | bytes 388
  147.7 72.6 %copy-start = (s32[4,1]{0,1:T(1,128)S(1)}, s32[4,1]{0,1:T(1,128)}, u32[]{:S(2)}) copy-start(s32[4,1]{0,1:T(1,128)} %param.12) | copy-start | bytes 52
  214.3 118.2 %all-to-all-start.2 = ((bf16[16,2,32768]{2,1,0:T(2,128)(2,1)}), bf16[16,2,32768]{2,1,0:T(2,128)(2,1)}, u32[]{:S(2)}, u32[]{:S(2)}) async-start(bf16[16,2,32768]{2,1,0:T(2,128)(2,1)} %reshape.95), calls=%async_computation.2 | async-start | bytes 4194304 | tf_op jit(solution)/shard_map/all_to_all | solution.py:50
  431.1 12.3 %copy-start.1 = (s32[4]{0:T(128)S(1)}, s32[4]{0:T(128)}, u32[]{:S(2)}) copy-start(s32[4]{0:T(128)} %param.13) | copy-start | bytes 52
  435.9 54.9 %all-to-all-start.3 = ((bf16[64,64,256]{2,1,0:T(8,128)(2,1)}), bf16[64,64,256]{2,1,0:T(8,128)(2,1)S(1)}, u32[]{:S(2)}, u32[]{:S(2)}) async-start(bf16[64,64,256]{2,1,0:T(8,128)(2,1)} %copy.32), calls=%async_computation.3 | async-start | bytes 4194304 | tf_op jit(solution)/shard_map/all_to_all | solution.py:52
Sparse Core Ops, SparseCore 0:
  9.5 193.1 all-gather.2
where the time goes:
time: 512 us; the launch traced here: 509 us
  waiting for transfers between devices  158 us (31%)
  local copies, waits for them, and re-layouts  133 us (26%)
  other arithmetic  70.9 us (14%)
  matrix products  65.3 us (13%)
  blocking collectives  44.1 us (9%)
  starting transfers between devices  23.2 us (5%)
  between operations  14.2 us (3%)
    unnamed x22, local copies, waits for them, and re-layouts  75.4 us
    all_to_all x1, waiting for transfers between devices, shards(): lax.all_to_all(goal_values, 'goal', split_axis=2, concat_axis=0, tiled=True)  58.2 us
    all_to_all x1, waiting for transfers between devices, shards(): lax.all_to_all(goal_keys, 'goal', split_axis=2, concat_axis=0, tiled=True)  52 us
    all_to_all x1, waiting for transfers between devices, shards(): lax.all_to_all(attended, 'goal', split_axis=0, concat_axis=2, tiled=True)  47.3 us
    unnamed x2, other arithmetic  44.6 us
    all_gather x1, blocking collectives, shards(): goal_ids = lax.all_gather(tactic_goal[:, 0], 'goal', axis=0, tiled=True)  44.1 us
    dot_general x1, matrix products, attend_block(): jnp.einsum('thij,tjhd->tihd', weights, vals_tact, preferred_element_type=...  43.3 us
    sub x1, other arithmetic, attend_block(): powers = jnp.exp(scores - biggest)  14.6 us
  transfers between devices with their start and end apart: 5, of which 3 were waited for; matrix products, arithmetic and copies ran while one was open for 51% of the time, Pallas kernels for 0%

commit v1 on v0

--- a/solution.py
+++ b/solution.py
@@ -1,3 +1,4 @@
+import functools
 import math
 import jax
 import jax.numpy as jnp
@@ -5,6 +6,19 @@
 from jax.sharding import PartitionSpec as P
 
 DH = 64
+
+
+def _arrange_set(array_here, device_axis, ndim_at, along_dim):
+    v_next = jnp.split(array_here, lax.psum(1, axis_name=device_axis), axis=ndim_at)
+    local_now = jnp.stack(v_next, axis=0)
+    then = jnp.concatenate(
+        lax.all_to_all(local_now, split_axis=0, concat_axis=0, axis_name=device_axis),
+        axis=along_dim,
+    )
+    return then
+
+
+_pair_wires = functools.partial(_arrange_set, device_axis="goal", ndim_at=2, along_dim=0)
 
 
 def attend_block(query_block, keys_heads, values_heads, block_ids):
@@ -44,7 +58,7 @@
 def shards(queries, goal_keys, goal_values, out_weight, tactic_goal, tactic_len):
     goal_ids = lax.all_gather(tactic_goal[:, 0], "goal", axis=0, tiled=True)
     keys_heads, values_heads = (
-        lax.all_to_all(goal_keys, "goal", split_axis=2, concat_axis=0, tiled=True),
+        _pair_wires(goal_keys),
         lax.all_to_all(goal_values, "goal", split_axis=2, concat_axis=0, tiled=True),
     )
     query_heads = lax.all_to_all(queries, "goal", split_axis=2, concat_axis=0, tiled=True)

time: 512 us -> 493 us (0.963)
  other arithmetic: 70.9 us -> 49.1 us
  waiting for transfers between devices: 158 us -> 172 us
  local copies, waits for them, and re-layouts: 133 us -> 123 us
    all_to_all x1, waiting for transfers between devices: 58.2 us -> 80.7 us  [shards(): lax.all_to_all(goal_values, 'goal', split_axis=2, concat_axis=0, tiled=True)]
    unnamed x2 -> x1, other arithmetic: 44.6 us -> 22.9 us
    all_to_all x1, waiting for transfers between devices: 52 us -> 43.2 us  [_arrange_set(): lax.all_to_all(local_now, split_axis=0, concat_axis=0, axis_name=device_a...]
    unnamed x22 -> x35, local copies, waits for them, and re-layouts: 75.4 us -> 66.9 us
  transfers between devices with their start and end apart: 5 -> 5, of which waited for: 3 -> 3; matrix products, arithmetic and copies ran while one was open for 51% -> 46% of each run, Pallas kernels for 0% -> 0%
where the time goes in v1:
time: 493 us; the launch traced here: 490 us
  waiting for transfers between devices  172 us (35%)
  local copies, waits for them, and re-layouts  123 us (25%)
  matrix products  65.2 us (13%)
  other arithmetic  49.1 us (10%)
  blocking collectives  44.1 us (9%)
  starting transfers between devices  23.2 us (5%)
  between operations  14.1 us (3%)
    all_to_all x1, waiting for transfers between devices, shards(): lax.all_to_all(goal_values, 'goal', split_axis=2, concat_axis=0, tiled=True)  80.7 us
    unnamed x35, local copies, waits for them, and re-layouts  66.9 us
    all_to_all x1, waiting for transfers between devices, shards(): lax.all_to_all(attended, 'goal', split_axis=0, concat_axis=2, tiled=True)  47.3 us
    all_gather x1, blocking collectives, shards(): goal_ids = lax.all_gather(tactic_goal[:, 0], 'goal', axis=0, tiled=True)  44.1 us
    all_to_all x1, waiting for transfers between devices, _arrange_set(): lax.all_to_all(local_now, split_axis=0, concat_axis=0, axis_name=device_a...  43.2 us
    dot_general x1, matrix products, attend_block(): jnp.einsum('thij,tjhd->tihd', weights, vals_tact, preferred_element_type=...  43.2 us
    unnamed x1, other arithmetic  22.9 us
    sub x1, other arithmetic, attend_block(): powers = jnp.exp(scores - biggest)  14.5 us
  transfers between devices with their start and end apart: 5, of which 3 were waited for; matrix products, arithmetic and copies ran while one was open for 46% of the time, Pallas kernels for 0%

profile of v1, /device:TPU:13, one launch (start us, length us, event | category | flops | bytes accessed | tf_op | source)
XLA Modules:
  0.0 490.3 jit_solution(16885261915778038758)
XLA Ops:
  6.5 0.7 all-gather.3.cloned.1.call-update
  7.3 1.6 bitcast_dynamic-update-slice_fusion.15
  8.8 1.6 bitcast_dynamic-update-slice_fusion.14
  10.4 1.6 bitcast_dynamic-update-slice_fusion.13
  12.0 1.6 bitcast_dynamic-update-slice_fusion.12
  13.5 1.6 bitcast_dynamic-update-slice_fusion.11
  15.1 0.7 bitcast_dynamic-update-slice_fusion.10
  15.7 0.7 bitcast_dynamic-update-slice_fusion.9
  16.4 0.7 bitcast_dynamic-update-slice_fusion.8
  17.1 0.7 bitcast_dynamic-update-slice_fusion.7
  17.7 0.7 bitcast_dynamic-update-slice_fusion.6
  18.4 0.7 bitcast_dynamic-update-slice_fusion.5
  19.1 0.7 bitcast_dynamic-update-slice_fusion.4
  19.8 0.7 bitcast_dynamic-update-slice_fusion.3
  20.4 0.7 bitcast_dynamic-update-slice_fusion.2
  21.1 0.7 bitcast_dynamic-update-slice_fusion.1
  21.8 0.7 bitcast_dynamic-update-slice_fusion
  22.4 6.6 %all-to-all-start.1 = ((bf16[16,1,256,256]{3,2,1,0:T(8,128)(2,1)}), bf16[16,1,256,256]{3,2,1,0:T(8,128)(2,1)S(1)}, u32[]{:S(2)}, u32[]{:S(2)}) async-start(bf16[16,1,256,256]{3,2,1,0:T(8,128)(2,1)} %bitcast_dynamic-update-slice_fusion), calls=%async_computation.1 | async-start | bytes 4194304 | tf_op jit(solution)/shard_map/all_to_all | solution.py:15
  29.0 10.1 %copy.20 = bf16[1,256,4096]{1,0,2:T(2,128)(2,1)} copy(bf16[1,256,4096]{2,1,0:T(8,128)(2,1)} %param.10) | data formatting | bytes 4194304 | tf_op args[2]
  39.5 22.9 %reduce = bf16[4096,256]{1,0:T(8,128)(2,1)} reduce(bf16[4096,1,256]{2,1,0:T(2,128)(2,1)} %bitcast.85, bf16[]{:T(256)} %broadcast.32), dimensions={1}, to_apply=%bitcast.73.reduce_sub_computation | reduce | bytes 4194306
  62.5 4.0 reshape.95
  66.4 43.2 %all-to-all-done.1 = bf16[16,1,256,256]{3,2,1,0:T(8,128)(2,1)S(1)} async-done(((bf16[16,1,256,256]{3,2,1,0:T(8,128)(2,1)}), bf16[16,1,256,256]{3,2,1,0:T(8,128)(2,1)S(1)}, u32[]{:S(2)}, u32[]{:S(2)}) %all-to-all-start.1) | async-done | bytes 2097184 | tf_op jit(solution)/shard_map/all_to_all | solution.py:15
  109.6 4.3 all-to-all-start
  114.0 6.9 %copy.24 = bf16[4,64,4096]{1,0,2:T(4,128)(2,1)} copy(bf16[4,64,4096]{2,1,0:T(8,128)(2,1)} %param.8) | data formatting | bytes 4194304 | tf_op args[0]
  120.9 7.5 %reshape.97 = bf16[16,2,32768]{2,1,0:T(2,128)(2,1)} reshape(bf16[4096,4,64]{2,1,0:T(4,128)(2,1)} %bitcast.88) | data formatting | bytes 4194304
  128.4 80.7 %all-to-all-done = bf16[16,2,32768]{2,1,0:T(2,128)(2,1)} async-done(((bf16[16,2,32768]{2,1,0:T(2,128)(2,1)}), bf16[16,2,32768]{2,1,0:T(2,128)(2,1)}, u32[]{:S(2)}, u32[]{:S(2)}) %all-to-all-start) | async-done | bytes 2097184 | tf_op jit(solution)/shard_map/all_to_all | solution.py:62
  209.1 4.7 all-to-all-start.2
  215.2 44.1 %all-reduce = s32[64]{0:T(128)S(1)} all-reduce(s32[64]{0:T(128)S(1)} %bitcast_dynamic-update-slice_fusion.16), channel_id=2, replica_groups=mesh['groups'=2,'goal'=16] {'goal'}, use_global_device_ids=true, to_apply=%add | all-reduce | flops 64 | bytes 512 | tf_op jit(solution)/shard_map/all_gather | solution.py:59
  259.3 10.4 %reshape.96 = bf16[4096,1,256]{2,1,0:T(2,128)(2,1)} reshape(bf16[16,2,32768]{2,1,0:T(2,128)(2,1)} %all-to-all-done) | data formatting | bytes 4194304
  269.7 3.9 copy.29
  273.6 3.9 copy.21
  277.5 5.5 %gather_fusion.1 = bf16[64,256,256]{2,1,0:T(8,128)(2,1)} fusion(bf16[16,256,256]{2,1,0:T(8,128)(2,1)S(1)} %bitcast.83, s32[1024]{0:T(1024)S(1)} %pad_clamp_fusion), kind=kCustom, calls=%fused_computation.1.clone | custom fusion | bytes 16777472 | tf_op jit(solution)/shard_map/while/body/eval_jaxpr/jit(_take)/gather | solution.py:29
  283.0 7.1 %gather_fusion = bf16[64,256,256]{2,1,0:T(8,128)(2,1)} fusion(bf16[16,256,256]{2,1,0:T(8,128)(2,1)} %bitcast.84, s32[1024]{0:T(1024)S(1)} %pad_clamp_fusion), kind=kCustom, calls=%fused_computation.clone | custom fusion | bytes 16777472 | tf_op jit(solution)/shard_map/while/body/eval_jaxpr/jit(_take)/gather | solution.py:30
  290.1 11.6 %broadcast_select_fusion = (bf16[64,256,256]{2,1,0:T(8,128)(2,1)}, bf16[64,256,256]{2,1,0:T(8,128)(2,1)}) fusion(bf16[64,256,256]{2,1,0:T(8,128)(2,1)} %gather_fusion.1, pred[64]{0:T(512)(128)(4,1)S(1)} %compare_and_fusion, bf16[64,256,256]{2,1,0:T(8,128)(2,1)} %gather_fusion), kind=kLoop, calls=%fused_computation.9 | loop fusion | flops 8388608 | bytes 33554496 | tf_op jit(solution)/shard_map/while/body/eval_jaxpr/jit(_take)/select_n | solution.py:29
  301.7 11.9 %copy.23 = bf16[64,256,256]{1,2,0:T(8,128)(2,1)} copy(bf16[64,256,256]{2,1,0:T(8,128)(2,1)} %get-tuple-element.16) | data formatting | bytes 16777216 | tf_op jit(solution)/shard_map/while/body/eval_jaxpr/jit(_take)/select_n | solution.py:29
  313.7 7.5 %reshape.98 = bf16[4096,4,64]{2,1,0:T(4,128)(2,1)} reshape(bf16[16,2,32768]{2,1,0:T(2,128)(2,1)} %all-to-all-done.2) | data formatting | bytes 4194304
  321.1 5.4 %copy.25 = bf16[4,64,16,256]{3,1,0,2:T(8,128)(2,1)S(1)} copy(bf16[4,64,16,256]{1,0,3,2:T(4,128)(2,1)} %bitcast.87) | data formatting | bytes 4194304 | tf_op jit(solution)/shard_map/all_to_all | solution.py:64
  326.5 3.3 reshape.64
  329.7 11.9 %copy.22 = bf16[64,256,256]{1,2,0:T(8,128)(2,1)} copy(bf16[64,256,256]{2,1,0:T(8,128)(2,1)} %get-tuple-element.17) | data formatting | bytes 16777216 | tf_op jit(solution)/shard_map/while/body/eval_jaxpr/jit(_take)/select_n | solution.py:30
  341.7 12.7 %fusion.6 = f32[64,4,256,64]{2,3,1,0:T(8,128)} fusion(bf16[64,256,4,64]{1,3,2,0:T(8,128)(2,1)} %bitcast.82, bf16[64,64,4,64]{3,2,1,0:T(4,128)(2,1)} %reshape.64), kind=kOutput, calls=%fused_computation.11 | convolution fusion | flops 536870912 | bytes 27262976 | tf_op jit(solution)/shard_map/while/body/eval_jaxpr/tihd,tjhd->thij/dot_general | solution.py:32
  354.4 14.5 %fusion.18 = f32[64,4,64]{2,1,0:T(4,128)S(1)} fusion(f32[64,4,256,64]{2,3,1,0:T(8,128)} %fusion.6), kind=kOutput, calls=%fused_computation.41 | output fusion | flops 8388863 | bytes 16842752 | tf_op jit(solution)/shard_map/while/body/eval_jaxpr/sub | solution.py:36
  368.9 43.2 %fusion.8 = bf16[64,4,64,64]{3,2,1,0:T(8,128)(2,1)} fusion(bf16[64,256,4,64]{1,3,2,0:T(8,128)(2,1)} %bitcast.91, f32[64,4,64]{2,1,0:T(4,128)S(1)} %fusion.18, f32[64,4,256,64]{2,3,1,0:T(8,128)} %fusion.6), kind=kOutput, calls=%fused_computation.13 | convolution fusion | flops 550519040 | bytes 27328512 | tf_op jit(solution)/shard_map/while/body/eval_jaxpr/thij,tjhd->tihd/dot_general | solution.py:38
  412.1 4.8 copy.27
  416.9 7.7 %all-to-all-start.3 = ((bf16[64,64,256]{2,1,0:T(8,128)(2,1)}), bf16[64,64,256]{2,1,0:T(8,128)(2,1)S(1)}, u32[]{:S(2)}, u32[]{:S(2)}) async-start(bf16[64,64,256]{2,1,0:T(8,128)(2,1)} %copy.27), calls=%async_computation.3 | async-start | bytes 4194304 | tf_op jit(solution)/shard_map/all_to_all | solution.py:66
  424.7 47.3 %all-to-all-done.3 = bf16[64,64,256]{2,1,0:T(8,128)(2,1)S(1)} async-done(((bf16[64,64,256]{2,1,0:T(8,128)(2,1)}), bf16[64,64,256]{2,1,0:T(8,128)(2,1)S(1)}, u32[]{:S(2)}, u32[]{:S(2)}) %all-to-all-start.3) | async-done | bytes 2097184 | tf_op jit(solution)/shard_map/all_to_all | solution.py:66
  471.9 1.2 copy.28
  473.1 0.9 copy.30
  474.1 9.3 %convolution_convert_fusion = bf16[256,2048]{1,0:T(8,128)(2,1)} fusion(bf16[4096,2048]{1,0:T(8,128)(2,1)} %all-gather.3.cloned.1.call-done, bf16[256,4096]{1,0:T(8,128)(2,1)S(1)} %bitcast.95, pred[256]{0:T(512)(128)(4,1)S(1)} %lt.30), kind=kOutput, calls=%fused_computation.14 | convolution fusion | flops 4296540160 | bytes 19923200 | tf_op jit(solution)/shard_map/dot_general | solution.py:72
  (20 shorter events, 1.4 us)
Async XLA Ops:
  6.5 8.5 %copy-start = (bf16[1,256,4096]{2,1,0:T(8,128)(2,1)S(1)}, bf16[1,256,4096]{2,1,0:T(8,128)(2,1)}, u32[]{:S(2)}) copy-start(bf16[1,256,4096]{2,1,0:T(8,128)(2,1)} %param.9) | copy-start | bytes 6291460
  6.5 467.6 %all-gather.3.cloned.1.call-start = ((), (), s32[]{:S(2)}) async-start(), calls=%async_computation.4 | async-start | bytes 17825792 | tf_op jit(solution)/shard_map/all_gather | solution.py:74
  22.4 87.2 %all-to-all-start.1 = ((bf16[16,1,256,256]{3,2,1,0:T(8,128)(2,1)}), bf16[16,1,256,256]{3,2,1,0:T(8,128)(2,1)S(1)}, u32[]{:S(2)}, u32[]{:S(2)}) async-start(bf16[16,1,256,256]{3,2,1,0:T(8,128)(2,1)} %bitcast_dynamic-update-slice_fusion), calls=%async_computation.1 | async-start | bytes 4194304 | tf_op jit(solution)/shard_map/all_to_all | solution.py:15
  109.6 99.5 %all-to-all-start = ((bf16[16,2,32768]{2,1,0:T(2,128)(2,1)}), bf16[16,2,32768]{2,1,0:T(2,128)(2,1)}, u32[]{:S(2)}, u32[]{:S(2)}) async-start(bf16[16,2,32768]{2,1,0:T(2,128)(2,1)} %reshape.95), calls=%async_computation | async-start | bytes 4194304 | tf_op jit(solution)/shard_map/all_to_all | solution.py:62
  128.4 85.4 %copy-start.3 = (u32[32]{0:T(128)S(1)}, u32[32]{0:T(128)}, u32[]{:S(2)}) copy-start(u32[32]{0:T(128)} %constant.37) | copy-start | bytes 388
  128.4 86.7 %copy-start.1 = (s32[4,1]{0,1:T(1,128)S(1)}, s32[4,1]{0,1:T(1,128)}, u32[]{:S(2)}) copy-start(s32[4,1]{0,1:T(1,128)} %param.12) | copy-start | bytes 52
  209.1 104.5 %all-to-all-start.2 = ((bf16[16,2,32768]{2,1,0:T(2,128)(2,1)}), bf16[16,2,32768]{2,1,0:T(2,128)(2,1)}, u32[]{:S(2)}, u32[]{:S(2)}) async-start(bf16[16,2,32768]{2,1,0:T(2,128)(2,1)} %reshape.97), calls=%async_computation.2 | async-start | bytes 4194304 | tf_op jit(solution)/shard_map/all_to_all | solution.py:64
  416.9 7.7 %copy-start.2 = (s32[4]{0:T(128)S(1)}, s32[4]{0:T(128)}, u32[]{:S(2)}) copy-start(s32[4]{0:T(128)} %param.13) | copy-start | bytes 52
  416.9 55.1 %all-to-all-start.3 = ((bf16[64,64,256]{2,1,0:T(8,128)(2,1)}), bf16[64,64,256]{2,1,0:T(8,128)(2,1)S(1)}, u32[]{:S(2)}, u32[]{:S(2)}) async-start(bf16[64,64,256]{2,1,0:T(8,128)(2,1)} %copy.27), calls=%async_computation.3 | async-start | bytes 4194304 | tf_op jit(solution)/shard_map/all_to_all | solution.py:66
Sparse Core Ops, SparseCore 0:
  9.5 202.2 all-gather.2
